TPU v7x, 512 devices: a whole 4x4x16 slice. The times are simulated.
512 devices in a mesh: vocab: 128 (over x, z, core), batch: 4 (over y).
Axes of the slice: x: 4, y: 4, z: 16, core: 2. Of those that a mesh axis runs over, the one named last changes fastest.
Arguments:
- hidden: bfloat16 [4096, 1024], P(('vocab', 'batch'))
- embedding: bfloat16 [131072, 1024], P('vocab')
- block_counts: int32 [1024], P('vocab'), may hold values from 1 to 4095
- lang_blocks: int32 [200, 64], replicated, may hold values from -1 to 1023, as said below
- sent_lang: int32 [64], replicated, may hold values from 0 to 199
- targets: int32 [4096], replicated, may hold values from 0 to 131071, as said below
Outputs:
- token_loss: float32 [4096], P(('vocab', 'batch'))
- grad_embed: bfloat16 [131072, 1024], P(('vocab', 'batch'))
Inputs may be any that keep to these rules, and one draw needn't show every extreme that they name: `lang_blocks`: each list holds distinct block numbers and then -1 padding; the first entry of every list is block 0; at least 16 entries are blocks, and some language fills all 64 entries. `targets`: the target of token t lies in a block listed for the language of sentence t // 64.
All inputs are finite; a program needn't handle non-finite values.
Results may differ from a plain program's by a relative error of at most 0.0075.
Values may be sent and summed in bfloat16 or wider, within the bound.
A program may use at most 64 MiB of HBM per device.

v0:
```python
import jax
import jax.numpy as jnp
from jax import lax
from jax.sharding import PartitionSpec as P

SEQ = 64
masked_fill = -1e30


def body(hidden, embedding, block_counts, lang_blocks, sent_lang, targets):
    tok_dev = hidden.shape[0]
    vocab_count = lax.axis_size("vocab")
    batch_count = lax.axis_size("batch")
    vocab_index = lax.axis_index("vocab")
    batch_index = lax.axis_index("batch")
    local_rows = embedding.shape[0]
    local_blocks = block_counts.shape[0]
    block_width = local_rows // local_blocks
    gathered = lax.all_gather(hidden, "vocab", axis=0, tiled=True)
    token_count = gathered.shape[0]
    token_ids = (
        (jnp.arange(vocab_count, dtype=jnp.int32)[:, None] * batch_count + batch_index) * tok_dev
        + jnp.arange(tok_dev, dtype=jnp.int32)[None, :]
    ).reshape(-1)
    target_ids = lax.dynamic_index_in_dim(
        targets.reshape(vocab_count, batch_count, tok_dev), batch_index, 1, keepdims=False
    ).reshape(-1)
    sentence = token_ids // SEQ
    sentence_hit = sentence[:, None] == jnp.arange(sent_lang.shape[0], dtype=jnp.int32)[None, :]
    token_language = jnp.sum(jnp.where(sentence_hit, sent_lang[None, :], 0), axis=1)
    block_ids = vocab_index * local_blocks + jnp.arange(local_blocks, dtype=jnp.int32)
    member = jnp.any(lang_blocks[:, :, None] == block_ids[None, None, :], axis=1).astype(
        jnp.float32
    )
    language_hit = (
        token_language[:, None] == jnp.arange(lang_blocks.shape[0], dtype=jnp.int32)[None, :]
    ).astype(jnp.float32)
    allowed = jnp.dot(language_hit, member, precision=lax.Precision.HIGHEST) > 0.5
    allowed_cells = allowed[:, :, None]
    raw_scores = lax.dot_general(
        gathered, embedding, (((1,), (1,)), ((), ())), preferred_element_type=jnp.float32
    )
    log_sampling = jnp.log(block_counts.astype(jnp.float32))
    logits = (
        raw_scores.reshape(token_count, local_blocks, block_width) - log_sampling[None, :, None]
    )
    masked = jnp.where(allowed_cells, logits, masked_fill)
    word_ids = (vocab_index * local_rows + jnp.arange(local_rows, dtype=jnp.int32)).reshape(
        local_blocks, block_width
    )
    is_target = word_ids[None, :, :] == target_ids[:, None, None]
    local_peak = jnp.max(masked, axis=(1, 2))
    local_target = jnp.sum(jnp.where(is_target, logits, 0.0), axis=(1, 2))
    peak_value = lax.pmax(local_peak, "vocab")
    local_total = jnp.sum(
        jnp.where(allowed_cells, jnp.exp(masked - peak_value[:, None, None]), 0.0), axis=(1, 2)
    )
    denominator, target_logit = lax.psum((local_total, local_target), "vocab")
    log_total = peak_value + jnp.log(denominator)
    every_loss = log_total - target_logit
    token_loss = lax.dynamic_slice_in_dim(every_loss, vocab_index * tok_dev, tok_dev, 0)
    softmax_weights = jnp.where(allowed_cells, jnp.exp(logits - log_total[:, None, None]), 0.0)
    grad_logits = (
        (softmax_weights - is_target.astype(jnp.float32))
        .astype(jnp.bfloat16)
        .reshape(token_count, local_rows)
    )
    partial_value = lax.dot_general(
        grad_logits, gathered, (((0,), (0,)), ((), ())), preferred_element_type=jnp.float32
    )
    rounded_terms = partial_value.astype(jnp.bfloat16)
    grad_embed = (
        lax.psum_scatter(rounded_terms, "batch", scatter_dimension=0, tiled=True)
        .astype(jnp.float32)
        .astype(jnp.bfloat16)
    )
    return (token_loss, grad_embed)


def solution(mesh):
    in_specs = (P(("vocab", "batch"), None), P("vocab", None), P("vocab"), P(), P(), P())
    out_specs = (P(("vocab", "batch")), P(("vocab", "batch"), None))
    return jax.shard_map(body, mesh=mesh, in_specs=in_specs, out_specs=out_specs, check_vma=False)
```

profile of v0, /device:TPU:1, one launch (start us, length us, event | category | flops | bytes accessed | tf_op | source)
XLA Modules:
  0.0 706.7 jit_solution(17756853080807426681)
XLA Ops:
  7.2 0.0 copy-start
  7.2 0.0 all-gather.2.cloned.1.call-start
  7.2 0.7 all-gather.2.cloned.1.call-update
  7.9 0.0 reduce-scatter.2.cloned.1.call-start
  8.0 0.1 iota_add_fusion
  8.1 0.1 add.86
  8.2 1.1 reshape.84
  9.2 0.2 dynamic-slice_reduce_fusion
  9.4 0.1 eq.66
  9.6 0.8 select_reduce_fusion
  10.3 1.0 compare_reduce_fusion
  11.3 0.7 convert_log_fusion
  12.0 0.1 broadcast_bitcast_fusion
  12.1 0.4 convolution_compare_fusion
  12.4 144.3 %all-gather.2.cloned.1.call-done = bf16[1024,1024]{1,0:T(8,128)(2,1)} async-done(((bf16[8,1024]{1,0:T(8,128)(2,1)}), bf16[1024,1024]{1,0:T(8,128)(2,1)}) %all-gather.2.cloned.1.call-update) | async-done | bytes 2097168 | tf_op jit(solution)/shard_map/all_gather | solution.py:19
  156.7 0.0 copy-done
  156.7 5.9 fusion.4
  162.6 246.4 %pmax.7 = f32[1024]{0:T(1024)S(1)} all-reduce(f32[1024]{0:T(1024)S(1)} %get-tuple-element.8), channel_id=1, replica_groups=mesh['vocab'=128,'batch'=4] {'vocab'}, use_global_device_ids=true, to_apply=%region_3.4 | all-reduce | flops 1024 | bytes 8192 | tf_op jit(solution)/shard_map/pmax | solution.py:54
  409.0 3.3 fusion
  412.3 254.4 %all-reduce = (f32[1024]{0:T(1024)S(1)}, f32[1024]{0:T(1024)S(1)}) all-reduce(f32[1024]{0:T(1024)S(1)} %get-tuple-element.3, f32[1024]{0:T(1024)S(1)} %get-tuple-element.2), channel_id=1, replica_groups=mesh['vocab'=128,'batch'=4] {'vocab'}, use_global_device_ids=true, to_apply=%region_5.6 | all-reduce | flops 2048 | bytes 16384 | tf_op jit(solution)/shard_map/psum | solution.py:58
  666.7 0.0 copy-start.1
  666.7 3.2 fusion.2
  669.9 0.0 copy-done.1
  669.9 3.7 convolution_convert_fusion
  673.6 0.0 reduce-scatter.2.cloned.1.call-update
  673.7 0.6 dynamic_slice.8
  674.3 25.6 %reduce-scatter.2.cloned.1.call-done = bf16[256,1024]{1,0:T(8,128)(2,1)} async-done(((bf16[1024,1024]{1,0:T(8,128)(2,1)}), bf16[256,1024]{1,0:T(8,128)(2,1)}) %reduce-scatter.2.cloned.1.call-update) | async-done | bytes 524304 | tf_op jit(solution)/shard_map/reduce_scatter | solution.py:73
  (5 shorter events, 0.0 us)
Async XLA Ops:
  7.2 149.5 %copy-start = (bf16[1024,1024]{1,0:T(8,128)(2,1)S(1)}, bf16[1024,1024]{1,0:T(8,128)(2,1)}, u32[]{:S(2)}) copy-start(bf16[1024,1024]{1,0:T(8,128)(2,1)} %param.7) | copy-start | bytes 6291460
  7.2 149.5 %all-gather.2.cloned.1.call-start = ((), (), s32[]{:S(2)}) async-start(), calls=%async_computation.1 | async-start | bytes 2113536 | tf_op jit(solution)/shard_map/all_gather | solution.py:19
  7.9 691.9 %reduce-scatter.2.cloned.1.call-start = ((), (), s32[]{:S(2)}) async-start(), calls=%async_computation.2 | async-start | bytes 2621440 | tf_op jit(solution)/shard_map/reduce_scatter | solution.py:73
  666.7 3.2 copy-start.1
Sparse Core Ops, SparseCore 0:
  11.1 145.4 all-gather.1
  673.8 26.0 reduce-scatter.1
where the time goes:
time: 707 us
  blocking collectives  501 us (71%)
  waiting for transfers between devices  171 us (24%)
  between operations  14.2 us (2%)
  matrix products  9.95 us (1%)
  other arithmetic  9.04 us (1%)
    psum x1, blocking collectives, body(): denominator, target_logit = lax.psum((local_total, local_target), 'vocab')  254 us
    pmax x1, blocking collectives, body(): peak_value = lax.pmax(local_peak, 'vocab')  246 us
    all_gather x1, waiting for transfers between devices, body(): gathered = lax.all_gather(hidden, 'vocab', axis=0, tiled=True)  144 us
    reduce_scatter x1, waiting for transfers between devices, body(): lax.psum_scatter(rounded_terms, 'batch', scatter_dimension=0, tiled=True)  25.6 us
  transfers between devices with their start and end apart: 2, of which 2 were waited for; matrix products, arithmetic and copies ran while one was open for 1% of the time, Pallas kernels for 0%

commit v1 on v0

--- a/solution.py
+++ b/solution.py
@@ -16,7 +16,9 @@
     local_rows = embedding.shape[0]
     local_blocks = block_counts.shape[0]
     block_width = local_rows // local_blocks
-    gathered = lax.all_gather(hidden, "vocab", axis=0, tiled=True)
+    gathered = jnp.concatenate(
+        lax.all_to_all(jnp.stack([hidden] * lax.axis_size("vocab")), "vocab", 0, 0), axis=0
+    )
     token_count = gathered.shape[0]
     token_ids = (
         (jnp.arange(vocab_count, dtype=jnp.int32)[:, None] * batch_count + batch_index) * tok_dev

time: 707 us -> 678 us (0.959)
  waiting for transfers between devices: 171 us -> 123 us
  starting transfers between devices: 0.08 us -> 20.9 us
    all_gather x1 -> x0, waiting for transfers between devices: 144 us -> none  [body(): gathered = lax.all_gather(hidden, 'vocab', axis=0, tiled=True)]
    all_to_all x0 -> x1, waiting for transfers between devices: none -> 97.2 us  [body(): lax.all_to_all(jnp.stack([hidden] * lax.axis_size('vocab')), 'vocab', 0, 0)]
    all_to_all x0 -> x1, starting transfers between devices: none -> 20.9 us  [body(): lax.all_to_all(jnp.stack([hidden] * lax.axis_size('vocab')), 'vocab', 0, 0)]
  transfers between devices with their start and end apart: 2 -> 2, of which waited for: 2 -> 2; matrix products, arithmetic and copies ran while one was open for 1% -> 0% of each run, Pallas kernels for 0% -> 0%
where the time goes in v1:
time: 678 us
  blocking collectives  498 us (73%)
  waiting for transfers between devices  123 us (18%)
  starting transfers between devices  20.9 us (3%)
  between operations  14.2 us (2%)
  matrix products  11.5 us (2%)
    psum x1, blocking collectives, body(): denominator, target_logit = lax.psum((local_total, local_target), 'vocab')  251 us
    pmax x1, blocking collectives, body(): peak_value = lax.pmax(local_peak, 'vocab')  247 us
    all_to_all x1, waiting for transfers between devices, body(): lax.all_to_all(jnp.stack([hidden] * lax.axis_size('vocab')), 'vocab', 0, 0)  97.2 us
    reduce_scatter x1, waiting for transfers between devices, body(): lax.psum_scatter(rounded_terms, 'batch', scatter_dimension=0, tiled=True)  25.8 us
    all_to_all x1, starting transfers between devices, body(): lax.all_to_all(jnp.stack([hidden] * lax.axis_size('vocab')), 'vocab', 0, 0)  20.9 us
  transfers between devices with their start and end apart: 2, of which 2 were waited for; matrix products, arithmetic and copies ran while one was open for 0% of the time, Pallas kernels for 0%

profile of v1, /device:TPU:1, one launch (start us, length us, event | category | flops | bytes accessed | tf_op | source)
XLA Modules:
  0.0 677.7 jit_solution(14025851545865825938)
XLA Ops:
  7.2 0.0 copy-start
  7.2 0.0 copy-start.2
  7.2 0.0 copy-start.3
  7.2 0.0 copy-start.1
  7.2 0.0 copy-start.4
  7.2 2.5 stack.2
  9.7 20.9 %all-to-all-start = ((bf16[128,8,1024]{2,1,0:T(8,128)(2,1)}), bf16[128,8,1024]{2,1,0:T(8,128)(2,1)}, u32[]{:S(2)}, u32[]{:S(2)}) async-start(bf16[128,8,1024]{2,1,0:T(8,128)(2,1)} %stack.2), calls=%async_computation | async-start | bytes 4194304 | tf_op jit(solution)/shard_map/all_to_all | solution.py:20
  30.6 0.0 reduce-scatter.2.cloned.1.call-start
  30.6 0.1 iota_add_fusion
  30.7 0.1 add.82
  30.8 0.0 copy-done.2
  30.8 0.3 reshape.76
  31.2 0.2 dynamic-slice_reduce_fusion
  31.4 0.1 eq.64
  31.5 0.0 copy-done.3
  31.5 0.1 select_reduce_fusion.2
  31.6 0.0 copy-done.1
  31.6 0.2 compare_reduce_fusion
  31.8 0.0 copy-done.4
  31.8 0.4 convolution_compare_fusion
  32.2 97.2 %all-to-all-done = bf16[128,8,1024]{2,1,0:T(8,128)(2,1)} async-done(((bf16[128,8,1024]{2,1,0:T(8,128)(2,1)}), bf16[128,8,1024]{2,1,0:T(8,128)(2,1)}, u32[]{:S(2)}, u32[]{:S(2)}) %all-to-all-start) | async-done | bytes 2097184 | tf_op jit(solution)/shard_map/all_to_all | solution.py:20
  129.3 0.0 copy-done
  129.3 5.9 select_reduce_fusion.1
  135.2 246.7 %pmax.7 = f32[1024]{0:T(1024)S(1)} all-reduce(f32[1024]{0:T(1024)S(1)} %get-tuple-element.8), channel_id=1, replica_groups=mesh['vocab'=128,'batch'=4] {'vocab'}, use_global_device_ids=true, to_apply=%region_3.4 | all-reduce | flops 1024 | bytes 8192 | tf_op jit(solution)/shard_map/pmax | solution.py:56
  382.0 3.3 fusion
  385.3 250.9 %all-reduce = (f32[1024]{0:T(1024)S(1)}, f32[1024]{0:T(1024)S(1)}) all-reduce(f32[1024]{0:T(1024)S(1)} %get-tuple-element.3, f32[1024]{0:T(1024)S(1)} %get-tuple-element.2), channel_id=1, replica_groups=mesh['vocab'=128,'batch'=4] {'vocab'}, use_global_device_ids=true, to_apply=%region_5.6 | all-reduce | flops 2048 | bytes 16384 | tf_op jit(solution)/shard_map/psum | solution.py:60
  636.2 3.0 fusion.2
  639.2 5.3 fusion.7
  644.5 0.0 reduce-scatter.2.cloned.1.call-update
  644.5 0.6 dynamic_slice.8
  645.1 25.8 %reduce-scatter.2.cloned.1.call-done = bf16[256,1024]{1,0:T(8,128)(2,1)} async-done(((bf16[1024,1024]{1,0:T(8,128)(2,1)}), bf16[256,1024]{1,0:T(8,128)(2,1)}) %reduce-scatter.2.cloned.1.call-update) | async-done | bytes 524304 | tf_op jit(solution)/shard_map/reduce_scatter | solution.py:75
  (6 shorter events, 0.0 us)
Async XLA Ops:
  7.2 122.2 %copy-start = (bf16[1024,1024]{1,0:T(8,128)(2,1)S(1)}, bf16[1024,1024]{1,0:T(8,128)(2,1)}, u32[]{:S(2)}) copy-start(bf16[1024,1024]{1,0:T(8,128)(2,1)} %param.7) | copy-start | bytes 6291460
  7.2 23.6 %copy-start.2 = (s32[4096]{0:T(1024)S(1)}, s32[4096]{0:T(1024)}, u32[]{:S(2)}) copy-start(s32[4096]{0:T(1024)} %param.11) | copy-start | bytes 49156
  7.2 24.3 %copy-start.3 = (s32[64]{0:T(128)S(1)}, s32[64]{0:T(128)}, u32[]{:S(2)}) copy-start(s32[64]{0:T(128)} %param.10) | copy-start | bytes 772
  7.2 24.4 %copy-start.1 = (s32[200,64]{0,1:T(8,128)S(1)}, s32[200,64]{0,1:T(8,128)}, u32[]{:S(2)}) copy-start(s32[200,64]{0,1:T(8,128)} %param.9) | copy-start | bytes 153604
  7.2 24.6 %copy-start.4 = (s32[8]{0:T(128)S(1)}, s32[8]{0:T(128)}, u32[]{:S(2)}) copy-start(s32[8]{0:T(128)} %param.8) | copy-start | bytes 100
  9.7 119.6 %all-to-all-start = ((bf16[128,8,1024]{2,1,0:T(8,128)(2,1)}), bf16[128,8,1024]{2,1,0:T(8,128)(2,1)}, u32[]{:S(2)}, u32[]{:S(2)}) async-start(bf16[128,8,1024]{2,1,0:T(8,128)(2,1)} %stack.2), calls=%async_computation | async-start | bytes 4194304 | tf_op jit(solution)/shard_map/all_to_all | solution.py:20
  30.6 640.3 %reduce-scatter.2.cloned.1.call-start = ((), (), s32[]{:S(2)}) async-start(), calls=%async_computation.2 | async-start | bytes 2621440 | tf_op jit(solution)/shard_map/reduce_scatter | solution.py:75
Sparse Core Ops, SparseCore 0:
  644.6 26.2 reduce-scatter.1
